TPU v7x, 32 devices: a whole 2x2x4 slice. The times are simulated.
32 devices in a mesh: grp: 2 (over x), ka: 16 (over z, y, core).
Axes of the slice: x: 2, y: 2, z: 4, core: 2. Of those that a mesh axis runs over, the one named last changes fastest.
Arguments:
- coefficients: bfloat16 [2, 512, 32768], P(None, 'ka'), may hold values from -768 to 768
- occ_weight: float32 [16, 32], replicated, may hold values from 0.02 to 1
- virt_weight: float32 [16, 32], replicated, may hold values from 0.02 to 1
- partner: int32 [32], P('grp'), parts along dimension 0, may hold values from 0 to 15, as said below
- points: int32 [1536], replicated, may hold values from 0 to 32767, as said below
Outputs:
- polarizability: float32 [4, 16, 384, 384], P('grp', 'ka'), parts along dimension 0
There are 2 independent parts, one for each index of `grp`. A program takes and returns all parts, laid end to end along the dimension named above; an argument that names none is the same for every part. Nothing has to cross between parts.
Inputs may be any that keep to these rules, and one draw needn't show every extreme that they name: 1536 distinct grid points. Every k-point is the partner of exactly one k-point.
All inputs are finite; a program needn't handle non-finite values.
Results may differ from a plain program's by a relative error of at most 0.0016.
Values may be sent and summed in bfloat16 or wider, within the bound.
A program may use at most 192 MiB of HBM per device.

v0:
```python
import functools
import math

import jax
import jax.numpy as jnp
from jax import lax
from jax.experimental import pallas as pl
from jax.experimental.pallas import tpu as pltpu
from jax.sharding import PartitionSpec as P

NG = 32
PLANE = NG * NG
GROUP = 8
VMEM_LIMIT = 56 * 1024 * 1024


def phase_rows(frequency, targets):
    angles = ((frequency * targets) % NG).astype(jnp.float32) * (2.0 * math.pi / NG)
    return jnp.cos(angles), jnp.sin(angles)


def orbital_kernel(chunk, pts_ref, coef_ref, out_ref, lhs, cos_hi, sin_hi, cos_lo, sin_lo, xcos, xsin, acc):
    step = pl.program_id(0)
    states = coef_ref.shape[1]
    count = pts_ref.shape[1]

    @pl.when(step == 0)
    def _():
        pts = pts_ref[...]
        frequency = lax.broadcasted_iota(jnp.int32, (NG, count), 0)
        norm = 1.0 / math.sqrt(NG**3)
        cos_x, sin_x = phase_rows(frequency, pts // PLANE)
        xcos[...] = cos_x * norm
        xsin[...] = sin_x * norm
        cos_y, sin_y = phase_rows(frequency, pts // NG % NG)
        cos_z, sin_z = phase_rows(frequency, pts % NG)
        for gy in range(NG):
            rows = slice(gy * NG, (gy + 1) * NG)
            cy, sy = cos_y[gy : gy + 1], sin_y[gy : gy + 1]
            cos_t = cy * cos_z - sy * sin_z
            sin_t = sy * cos_z + cy * sin_z
            high = cos_t.astype(jnp.bfloat16)
            cos_hi[rows] = high
            cos_lo[rows] = (cos_t - high.astype(jnp.float32)).astype(jnp.bfloat16)
            high = sin_t.astype(jnp.bfloat16)
            sin_hi[rows] = high
            sin_lo[rows] = (sin_t - high.astype(jnp.float32)).astype(jnp.bfloat16)
        acc[...] = jnp.zeros_like(acc)

    for j in range(GROUP):
        for c in range(2):
            start = (2 * j + c) * states
            lhs[start : start + states] = coef_ref[c, :, j * PLANE : (j + 1) * PLANE]

    def dot(table, low, cols):
        left = lhs[...]
        return jnp.dot(left, table[:, cols], preferred_element_type=jnp.float32) + jnp.dot(
            left, low[:, cols], preferred_element_type=jnp.float32
        )

    gx = pl.ds(pl.multiple_of(step * GROUP, GROUP), GROUP)
    for m in range(count // chunk):
        cols = slice(m * chunk, (m + 1) * chunk)
        by_cos = dot(cos_hi, cos_lo, cols)
        by_sin = dot(sin_hi, sin_lo, cols)
        pc, ps = xcos[gx, cols], xsin[gx, cols]
        real_sum, imag_sum = acc[0, :, cols], acc[1, :, cols]
        for j in range(GROUP):
            a = slice(2 * j * states, (2 * j + 1) * states)
            b = slice((2 * j + 1) * states, (2 * j + 2) * states)
            re = by_cos[a] - by_sin[b]
            im = by_sin[a] + by_cos[b]
            c, s = pc[j : j + 1], ps[j : j + 1]
            real_sum = real_sum + (re * c - im * s)
            imag_sum = imag_sum + (re * s + im * c)
        acc[0, :, cols] = real_sum
        acc[1, :, cols] = imag_sum

    @pl.when(step == pl.num_programs(0) - 1)
    def _():
        out_ref[...] = acc[...].astype(jnp.bfloat16)


def orbitals_at(coefficients, points):
    states = coefficients.shape[1]
    count = points.shape[0]
    chunk = 256 if count % 256 == 0 else 128
    table = pltpu.VMEM((PLANE, count), jnp.bfloat16)
    return pl.pallas_call(
        functools.partial(orbital_kernel, chunk),
        grid=(NG // GROUP,),
        out_shape=jax.ShapeDtypeStruct((2, states, count), jnp.bfloat16),
        in_specs=[
            pl.BlockSpec((1, count), lambda i: (0, 0)),
            pl.BlockSpec((2, states, GROUP * PLANE), lambda i: (0, 0, i)),
        ],
        out_specs=pl.BlockSpec((2, states, count), lambda i: (0, 0, 0)),
        scratch_shapes=[
            pltpu.VMEM((GROUP * 2 * states, PLANE), jnp.bfloat16),
            table, table, table, table,
            pltpu.VMEM((NG, count), jnp.float32),
            pltpu.VMEM((NG, count), jnp.float32),
            pltpu.VMEM((2, states, count), jnp.float32),
        ],
        compiler_params=pltpu.CompilerParams(vmem_limit_bytes=VMEM_LIMIT),
        name="orbitals",
    )(points.reshape(1, count), coefficients)


def polar_kernel(partner_ref, row_ref, col_ref, occ_ref, virt_ref, out_ref):
    kpoints, parts, bands, _ = row_ref.shape
    scaling = 1.0 / (bands * bands)
    dims = (((0,), (0,)), ((), ()))

    def density(k, weight_ref):
        rows = row_ref[k].astype(jnp.float32)
        weighted = (rows * weight_ref[k][None]).astype(jnp.bfloat16)
        cols = col_ref[k]
        right = jnp.concatenate([cols[0], cols[1]], axis=0)
        real_left = jnp.concatenate([weighted[0], weighted[1]], axis=0)
        imag_left = jnp.concatenate([weighted[1], -weighted[0]], axis=0)
        return (
            lax.dot_general(real_left, right, dims, preferred_element_type=jnp.float32),
            lax.dot_general(imag_left, right, dims, preferred_element_type=jnp.float32),
        )

    def step(k, carry):
        occ_real, occ_imag = density(k, occ_ref)
        virt_real, virt_imag = density(partner_ref[k], virt_ref)
        out_ref[0, 0] += (occ_real * virt_real + occ_imag * virt_imag) * scaling
        out_ref[1, 0] += (occ_imag * virt_real - occ_real * virt_imag) * scaling
        return carry

    out_ref[...] = jnp.zeros_like(out_ref)
    lax.fori_loop(0, kpoints, step, 0)


def polarizability(partner, row_side, col_side, occ_weight, virt_weight):
    row_len, col_len = row_side.shape[3], col_side.shape[3]
    vmem = pl.BlockSpec(memory_space=pltpu.VMEM)
    return pl.pallas_call(
        polar_kernel,
        out_shape=jax.ShapeDtypeStruct((2, 1, row_len, col_len), jnp.float32),
        in_specs=[pl.BlockSpec(memory_space=pltpu.SMEM), vmem, vmem, vmem, vmem],
        out_specs=vmem,
        compiler_params=pltpu.CompilerParams(vmem_limit_bytes=VMEM_LIMIT),
        name="polarizability",
    )(partner, row_side, col_side, occ_weight[:, :, None], virt_weight[:, :, None])


def body(coefficients, occ_weight, virt_weight, partner, points):
    devices = lax.axis_size("ka")
    groups = lax.axis_size("grp")
    col_blocks = min(16, max(4, devices // 8))
    row_blocks = devices // col_blocks
    kpoints, bands = occ_weight.shape
    point_count = points.shape[0]
    states = coefficients.shape[1]
    row_len = point_count // row_blocks
    col_len = point_count // col_blocks
    share = point_count // groups
    mine = lax.dynamic_slice_in_dim(points, lax.axis_index("grp") * share, share)
    orbitals = orbitals_at(coefficients, mine)
    orbitals = lax.all_gather(orbitals, "grp", axis=2, tiled=True)
    planes = [list(range(r * col_blocks, (r + 1) * col_blocks)) for r in range(row_blocks)]
    lines = [list(range(c, devices, col_blocks)) for c in range(col_blocks)]

    def split(count):
        return jnp.transpose(orbitals.reshape(2, states, count, -1), (2, 0, 1, 3))

    rows = split(row_blocks)
    rows = lax.all_to_all(rows, "ka", 0, 0, axis_index_groups=lines, tiled=True)
    rows = lax.all_gather(rows, "ka", axis=0, axis_index_groups=planes)
    rows = jnp.swapaxes(rows, 0, 1)
    cols = split(col_blocks)
    cols = lax.all_to_all(cols, "ka", 0, 0, axis_index_groups=planes, tiled=True)
    cols = lax.all_gather(cols, "ka", axis=0, axis_index_groups=lines)

    def by_kpoint(side, length):
        side = side.reshape(kpoints, devices // kpoints, 2, states, length)
        return jnp.swapaxes(side, 1, 2).reshape(kpoints, 2, bands, length)

    return polarizability(
        partner, by_kpoint(rows, row_len), by_kpoint(cols, col_len), occ_weight, virt_weight
    )


def solution(mesh):
    return jax.shard_map(
        body,
        mesh=mesh,
        in_specs=(P(None, "ka", None), P(), P(), P("grp"), P()),
        out_specs=P("grp", "ka", None, None),
        check_vma=False,
    )
```

profile of v0, /device:TPU:0, one launch (start us, length us, event | category | flops | bytes accessed | tf_op | source)
XLA Modules:
  0.0 84.5 jit_solution(6647748420140947895)
XLA Ops:
  0.0 0.0 copy-start
  0.0 0.0 copy-start.1
  0.0 0.8 dynamic_slice.3
  0.8 0.6 reshape.7.pts_ref
  1.4 18.5 %orbitals.1 = bf16[2,32,768]{2,1,0:T(8,128)(2,1)} custom-call(s32[1,768]{1,0:T(1,128)} %reshape.7.pts_ref, bf16[2,32,32768]{2,1,0:T(8,128)(2,1)} %coef_ref.1), custom_call_target="tpu_custom_call" | custom-call | tf_op jit(solution)/shard_map/orbitals/pallas_call | solution.py:89
  19.9 6.6 %all_gather.15 = bf16[2,32,1536]{2,1,0:T(8,128)(2,1)S(1)} all-gather(bf16[2,32,768]{2,1,0:T(8,128)(2,1)} %orbitals.1), channel_id=1, replica_groups=mesh['grp'=2,'ka'=16] {'grp'}, dimensions={2}, use_global_device_ids=true | all-gather | bytes 294912 | tf_op jit(solution)/shard_map/all_gather | solution.py:164
  26.6 0.7 copy.16
  27.3 3.4 %all-to-all-start.1 = ((bf16[4,2,32,384]{3,2,1,0:T(8,128)(2,1)}), bf16[4,2,32,384]{3,2,1,0:T(8,128)(2,1)S(1)}, u32[]{:S(2)}, u32[]{:S(2)}) async-start(bf16[4,2,32,384]{3,2,1,0:T(8,128)(2,1)} %copy.16), calls=%async_computation.1 | async-start | bytes 393216 | tf_op jit(solution)/shard_map/all_to_all | solution.py:176
  30.6 0.0 copy-done
  30.6 0.9 %copy.19.occ_ref = f32[16,32,1]{2,1,0:T(8,128)} copy(f32[16,32,1]{1,0,2:T(8,128)S(1)} %bitcast.10) | data formatting | bytes 4096 | tf_op jit(solution)/shard_map/broadcast_in_dim | solution.py:148
  31.5 0.0 copy-done.1
  31.5 0.9 %copy.20.virt_ref = f32[16,32,1]{2,1,0:T(8,128)} copy(f32[16,32,1]{1,0,2:T(8,128)S(1)} %bitcast.11) | data formatting | bytes 4096 | tf_op jit(solution)/shard_map/broadcast_in_dim | solution.py:148
  32.4 3.5 %all-to-all-done.1 = bf16[4,2,32,384]{3,2,1,0:T(8,128)(2,1)S(1)} async-done(((bf16[4,2,32,384]{3,2,1,0:T(8,128)(2,1)}), bf16[4,2,32,384]{3,2,1,0:T(8,128)(2,1)S(1)}, u32[]{:S(2)}, u32[]{:S(2)}) %all-to-all-start.1) | async-done | bytes 196640 | tf_op jit(solution)/shard_map/all_to_all | solution.py:176
  35.9 5.2 %all-to-all-start = ((bf16[4,2,32,384]{3,2,1,0:T(8,128)(2,1)}), bf16[4,2,32,384]{3,2,1,0:T(8,128)(2,1)S(1)}, u32[]{:S(2)}, u32[]{:S(2)}) async-start(bf16[4,2,32,384]{3,2,1,0:T(8,128)(2,1)} %copy.16), calls=%async_computation | async-start | bytes 393216 | tf_op jit(solution)/shard_map/all_to_all | solution.py:172
  41.1 21.2 %all-gather.1.col_ref = bf16[16,2,32,384]{3,2,1,0:T(8,128)(2,1)} all-gather(bf16[4,2,32,384]{3,2,1,0:T(8,128)(2,1)S(1)} %all-to-all-done.1), channel_id=3, replica_groups={{0,4,8,12},{1,5,9,13},{2,6,10,14},{3,7,11,15},{16,20,24,28},{17,21,25,2..., dimensions={0}, use_global_device_ids=true | all-gather | bytes 983040 | tf_op jit(solution)/shard_map/all_gather | solution.py:177
  62.3 0.0 all-to-all-done
  62.3 7.6 %all-gather = bf16[16,2,32,384]{3,2,1,0:T(8,128)(2,1)S(1)} all-gather(bf16[4,2,32,384]{3,2,1,0:T(8,128)(2,1)S(1)} %all-to-all-done), channel_id=2, replica_groups={{0,1,2,3},{4,5,6,7},{8,9,10,11},{12,13,14,15},{16,17,18,19},{20,21,22,2..., dimensions={0}, use_global_device_ids=true | all-gather | bytes 983040 | tf_op jit(solution)/shard_map/all_gather | solution.py:173
  69.9 1.0 %copy.17 = bf16[4,4,2,32,384]{4,3,2,0,1:T(8,128)(2,1)} copy(bf16[4,4,2,32,384]{4,3,2,1,0:T(8,128)(2,1)S(1)} %bitcast.8) | data formatting | bytes 1572864 | tf_op jit(solution)/shard_map/all_gather | solution.py:173
  70.9 13.6 %polarizability.1 = f32[2,1,384,384]{3,2,1,0:T(8,128)} custom-call(s32[16]{0:T(128)} %partner_ref.1, bf16[16,2,32,384]{3,2,1,0:T(8,128)(2,1)} %bitcast.7, bf16[16,2,32,384]{3,2,1,0:T(8,128)(2,1)} %all-gather.1.col_ref, f32[16,32,1]{2,1,0:T(8,128)} %copy.19.occ_ref, f32[16,32,1]{2,1,0:T(8,128)} %copy.20.virt_ref), custom_call_target="tpu_custom_call" | custom-call | tf_op jit(solution)/shard_map/polarizability/pallas_call | solution.py:141
  (1 shorter events, 0.0 us)
Async XLA Ops:
  0.0 30.6 %copy-start = (f32[16,32]{1,0:T(8,128)S(1)}, f32[16,32]{1,0:T(8,128)}, u32[]{:S(2)}) copy-start(f32[16,32]{1,0:T(8,128)} %param.6) | copy-start | bytes 6148
  0.0 31.5 %copy-start.1 = (f32[16,32]{1,0:T(8,128)S(1)}, f32[16,32]{1,0:T(8,128)}, u32[]{:S(2)}) copy-start(f32[16,32]{1,0:T(8,128)} %param.7) | copy-start | bytes 6148
  27.3 8.7 %all-to-all-start.1 = ((bf16[4,2,32,384]{3,2,1,0:T(8,128)(2,1)}), bf16[4,2,32,384]{3,2,1,0:T(8,128)(2,1)S(1)}, u32[]{:S(2)}, u32[]{:S(2)}) async-start(bf16[4,2,32,384]{3,2,1,0:T(8,128)(2,1)} %copy.16), calls=%async_computation.1 | async-start | bytes 393216 | tf_op jit(solution)/shard_map/all_to_all | solution.py:176
  35.9 26.3 %all-to-all-start = ((bf16[4,2,32,384]{3,2,1,0:T(8,128)(2,1)}), bf16[4,2,32,384]{3,2,1,0:T(8,128)(2,1)S(1)}, u32[]{:S(2)}, u32[]{:S(2)}) async-start(bf16[4,2,32,384]{3,2,1,0:T(8,128)(2,1)} %copy.16), calls=%async_computation | async-start | bytes 393216 | tf_op jit(solution)/shard_map/all_to_all | solution.py:172
where the time goes:
time: 84.9 us; the launch traced here: 84.5 us
  blocking collectives  35.4 us (42%)
  Pallas kernels  32.1 us (38%)
  starting transfers between devices  8.53 us (10%)
  local copies, waits for them, and re-layouts  4.88 us (6%)
  waiting for transfers between devices  3.55 us (4%)
    all_gather x1, blocking collectives, body(): cols = lax.all_gather(cols, 'ka', axis=0, axis_index_groups=lines)  21.2 us
    pallas_call x1, Pallas kernels, orbitals_at(): pl.pallas_call(functools.partial(orbital_kernel, chunk), grid=(NG // GROU...  18.5 us
    pallas_call x1, Pallas kernels, polarizability(): pl.pallas_call(polar_kernel, out_shape=jax.ShapeDtypeStruct((2, 1, row_le...  13.6 us
    all_gather x1, blocking collectives, body(): rows = lax.all_gather(rows, 'ka', axis=0, axis_index_groups=planes)  7.63 us
    all_gather x1, blocking collectives, body(): orbitals = lax.all_gather(orbitals, 'grp', axis=2, tiled=True)  6.65 us
    all_to_all x1, starting transfers between devices, body(): rows = lax.all_to_all(rows, 'ka', 0, 0, axis_index_groups=lines, tiled=True)  5.16 us
    all_to_all x1, waiting for transfers between devices, body(): lax.all_to_all(cols, 'ka', 0, 0, axis_index_groups=planes, tiled=True)  3.55 us
    all_to_all x1, starting transfers between devices, body(): lax.all_to_all(cols, 'ka', 0, 0, axis_index_groups=planes, tiled=True)  3.37 us
  transfers between devices with their start and end apart: 2, of which 1 were waited for; matrix products, arithmetic and copies ran while one was open for 2% of the time, Pallas kernels for 0%

commit v1 on v0

--- a/solution.py
+++ b/solution.py
@@ -22,11 +22,12 @@
 def orbital_kernel(chunk, pts_ref, coef_ref, out_ref, lhs, cos_hi, sin_hi, cos_lo, sin_lo, xcos, xsin, acc):
     step = pl.program_id(0)
     states = coef_ref.shape[1]
-    count = pts_ref.shape[1]
+    count = acc.shape[2]
 
     @pl.when(step == 0)
     def _():
-        pts = pts_ref[...]
+        start = pl.multiple_of(lax.axis_index("grp") * count, 128)
+        pts = pts_ref[:, pl.ds(start, count)]
         frequency = lax.broadcasted_iota(jnp.int32, (NG, count), 0)
         norm = 1.0 / math.sqrt(NG**3)
         cos_x, sin_x = phase_rows(frequency, pts // PLANE)
@@ -78,23 +79,26 @@
 
     @pl.when(step == pl.num_programs(0) - 1)
     def _():
-        out_ref[...] = acc[...].astype(jnp.bfloat16)
-
-
-def orbitals_at(coefficients, points):
+        blocks, _, _, length = out_ref.shape
+        for b in range(blocks):
+            out_ref[b] = acc[:, :, b * length : (b + 1) * length].astype(jnp.bfloat16)
+
+
+def orbitals_at(coefficients, points, count, length):
     states = coefficients.shape[1]
-    count = points.shape[0]
+    total = points.shape[0]
     chunk = 256 if count % 256 == 0 else 128
     table = pltpu.VMEM((PLANE, count), jnp.bfloat16)
+    out_shape = (count // length, 2, states, length)
     return pl.pallas_call(
         functools.partial(orbital_kernel, chunk),
         grid=(NG // GROUP,),
-        out_shape=jax.ShapeDtypeStruct((2, states, count), jnp.bfloat16),
+        out_shape=jax.ShapeDtypeStruct(out_shape, jnp.bfloat16),
         in_specs=[
-            pl.BlockSpec((1, count), lambda i: (0, 0)),
+            pl.BlockSpec((1, total), lambda i: (0, 0)),
             pl.BlockSpec((2, states, GROUP * PLANE), lambda i: (0, 0, i)),
         ],
-        out_specs=pl.BlockSpec((2, states, count), lambda i: (0, 0, 0)),
+        out_specs=pl.BlockSpec(out_shape, lambda i: (0, 0, 0, 0)),
         scratch_shapes=[
             pltpu.VMEM((GROUP * 2 * states, PLANE), jnp.bfloat16),
             table, table, table, table,
@@ -104,7 +108,138 @@
         ],
         compiler_params=pltpu.CompilerParams(vmem_limit_bytes=VMEM_LIMIT),
         name="orbitals",
-    )(points.reshape(1, count), coefficients)
+    )(points.reshape(1, total), coefficients)
+
+
+def exchange_kernel(groups, n, own_ref, rows, cols, blocks, local_sem, x_send, x_recv,
+                    r1_send, r1_recv, c1_send, c1_recv, r2_send, r2_recv,
+                    up_send, up_recv, down_send, down_recv):
+    me = lax.axis_index("ka")
+    g = lax.axis_index("grp")
+    line, place = me // n, me % n
+    held = own_ref.shape[0]
+
+    def turn(value, by):
+        return (value + by) % n
+
+    barrier = pltpu.get_barrier_semaphore()
+    for d in range(1, groups):
+        pl.semaphore_signal(barrier, inc=1, device_id={"grp": (g + d) % groups, "ka": me},
+                            device_id_type=pl.DeviceIdType.MESH)
+    for d in range(1, n):
+        for peer in (turn(line, d) * n + place, line * n + turn(place, d)):
+            pl.semaphore_signal(barrier, inc=1, device_id={"grp": g, "ka": peer},
+                                device_id_type=pl.DeviceIdType.MESH)
+    pl.semaphore_wait(barrier, groups - 1 + 2 * (n - 1))
+
+    pending = []
+
+    def send(src, dst, send_sem, recv_sem, peer, grp=None, when=None):
+        copy = pltpu.make_async_remote_copy(
+            src_ref=src, dst_ref=dst, send_sem=send_sem, recv_sem=recv_sem,
+            device_id={"grp": g if grp is None else grp, "ka": peer},
+            device_id_type=pl.DeviceIdType.MESH,
+        )
+        guarded(when, copy.start)
+        pending.append((when, copy.wait_send))
+
+    def arrive(dst, send_sem, recv_sem):
+        pltpu.make_async_remote_copy(
+            src_ref=dst, dst_ref=dst, send_sem=send_sem, recv_sem=recv_sem,
+            device_id={"grp": g, "ka": turn(line, 1) * n + place},
+            device_id_type=pl.DeviceIdType.MESH,
+        ).wait_recv()
+
+    def guarded(when, run):
+        if when is None:
+            run()
+        else:
+            pl.when(when)(run)
+
+    def share(grp):
+        return blocks.at[pl.ds(grp * held, held)]
+
+    for d in range(1, groups):
+        send(own_ref, share(g), x_send.at[d], x_recv.at[d], me, grp=(g + d) % groups)
+    keep = pltpu.make_async_copy(own_ref, share(g), local_sem.at[0])
+    keep.start()
+    keep.wait()
+    for d in range(1, groups):
+        arrive(share((g + groups - d) % groups), x_send.at[d], x_recv.at[d])
+
+    for d in range(1, n):
+        send(blocks.at[turn(line, d)], rows.at[me], r1_send.at[d], r1_recv.at[d],
+             turn(line, d) * n + place)
+        send(blocks.at[turn(place, d)], cols.at[me], c1_send.at[d], c1_recv.at[d],
+             line * n + turn(place, d))
+    own_row = pltpu.make_async_copy(blocks.at[line], rows.at[me], local_sem.at[1])
+    own_col = pltpu.make_async_copy(blocks.at[place], cols.at[me], local_sem.at[2])
+    own_row.start()
+    own_col.start()
+
+    above, below = line < n - 1, line > 0
+    for d in range(n):
+        slot = line * n + turn(place, n - d)
+        if d:
+            arrive(cols.at[slot], c1_send.at[d], c1_recv.at[d])
+        source = cols.at[slot] if d else blocks.at[place]
+        send(source, cols.at[slot], up_send.at[0, d], up_recv.at[0, d], me + n, when=above)
+        send(source, cols.at[slot], down_send.at[0, d], down_recv.at[0, d], me - n, when=below)
+        slot = turn(line, n - d) * n + place
+        if d:
+            arrive(rows.at[slot], r1_send.at[d], r1_recv.at[d])
+        source = rows.at[slot] if d else blocks.at[line]
+        for e in range(1, n):
+            send(source, rows.at[slot], r2_send.at[d, e], r2_recv.at[d, e],
+                 line * n + turn(place, e))
+
+    for t in range(1, n):
+        for d in range(n):
+            def from_below(t=t, d=d):
+                slot = (line - t) * n + turn(place, n - d)
+                arrive(cols.at[slot], up_send.at[t - 1, d], up_recv.at[t - 1, d])
+
+            def from_above(t=t, d=d):
+                slot = (line + t) * n + turn(place, n - d)
+                arrive(cols.at[slot], down_send.at[t - 1, d], down_recv.at[t - 1, d])
+
+            pl.when(line - t >= 0)(from_below)
+            if t < n - 1:
+                slot = jnp.maximum(line - t, 0) * n + turn(place, n - d)
+                send(cols.at[slot], cols.at[slot], up_send.at[t, d], up_recv.at[t, d], me + n,
+                     when=jnp.logical_and(line - t >= 0, above))
+            pl.when(line + t < n)(from_above)
+            if t < n - 1:
+                slot = jnp.minimum(line + t, n - 1) * n + turn(place, n - d)
+                send(cols.at[slot], cols.at[slot], down_send.at[t, d], down_recv.at[t, d], me - n,
+                     when=jnp.logical_and(line + t < n, below))
+
+    for d in range(n):
+        for e in range(1, n):
+            slot = turn(line, n - d) * n + turn(place, n - e)
+            arrive(rows.at[slot], r2_send.at[d, e], r2_recv.at[d, e])
+    own_row.wait()
+    own_col.wait()
+    for when, wait in pending:
+        guarded(when, wait)
+
+
+def exchange(own, groups, devices, n):
+    _, _, states, length = own.shape
+    anywhere = pl.BlockSpec(memory_space=pl.ANY)
+    side = jax.ShapeDtypeStruct((devices, 2, states, length), jnp.bfloat16)
+    sem = pltpu.SemaphoreType.DMA
+    rows, cols, _ = pl.pallas_call(
+        functools.partial(exchange_kernel, groups, n),
+        out_shape=[side, side, jax.ShapeDtypeStruct((n, 2, states, length), jnp.bfloat16)],
+        in_specs=[anywhere],
+        out_specs=[anywhere] * 3,
+        scratch_shapes=[sem((3,)), sem((groups,)), sem((groups,))]
+        + [sem((n,))] * 4 + [sem((n, n))] * 6,
+        compiler_params=pltpu.CompilerParams(collective_id=0, has_side_effects=True),
+        name="exchange",
+    )(own)
+    return rows, cols
 
 
 def polar_kernel(partner_ref, row_ref, col_ref, occ_ref, virt_ref, out_ref):
@@ -112,9 +247,15 @@
     scaling = 1.0 / (bands * bands)
     dims = (((0,), (0,)), ((), ()))
 
+    diagonal = lax.broadcasted_iota(jnp.int32, (bands, bands), 0) == lax.broadcasted_iota(
+        jnp.int32, (bands, bands), 1
+    )
+
     def density(k, weight_ref):
         rows = row_ref[k].astype(jnp.float32)
-        weighted = (rows * weight_ref[k][None]).astype(jnp.bfloat16)
+        weight = jnp.where(diagonal, weight_ref[pl.ds(k, 1), :], 0.0)
+        weight = jnp.sum(weight, axis=1, keepdims=True)
+        weighted = (rows * weight[None]).astype(jnp.bfloat16)
         cols = col_ref[k]
         right = jnp.concatenate([cols[0], cols[1]], axis=0)
         real_left = jnp.concatenate([weighted[0], weighted[1]], axis=0)
@@ -145,7 +286,7 @@
         out_specs=vmem,
         compiler_params=pltpu.CompilerParams(vmem_limit_bytes=VMEM_LIMIT),
         name="polarizability",
-    )(partner, row_side, col_side, occ_weight[:, :, None], virt_weight[:, :, None])
+    )(partner, row_side, col_side, occ_weight, virt_weight)
 
 
 def body(coefficients, occ_weight, virt_weight, partner, points):
@@ -158,23 +299,8 @@
     states = coefficients.shape[1]
     row_len = point_count // row_blocks
     col_len = point_count // col_blocks
-    share = point_count // groups
-    mine = lax.dynamic_slice_in_dim(points, lax.axis_index("grp") * share, share)
-    orbitals = orbitals_at(coefficients, mine)
-    orbitals = lax.all_gather(orbitals, "grp", axis=2, tiled=True)
-    planes = [list(range(r * col_blocks, (r + 1) * col_blocks)) for r in range(row_blocks)]
-    lines = [list(range(c, devices, col_blocks)) for c in range(col_blocks)]
-
-    def split(count):
-        return jnp.transpose(orbitals.reshape(2, states, count, -1), (2, 0, 1, 3))
-
-    rows = split(row_blocks)
-    rows = lax.all_to_all(rows, "ka", 0, 0, axis_index_groups=lines, tiled=True)
-    rows = lax.all_gather(rows, "ka", axis=0, axis_index_groups=planes)
-    rows = jnp.swapaxes(rows, 0, 1)
-    cols = split(col_blocks)
-    cols = lax.all_to_all(cols, "ka", 0, 0, axis_index_groups=planes, tiled=True)
-    cols = lax.all_gather(cols, "ka", axis=0, axis_index_groups=lines)
+    own = orbitals_at(coefficients, points, point_count // groups, row_len)
+    rows, cols = exchange(own, groups, devices, col_blocks)
 
     def by_kpoint(side, length):
         side = side.reshape(kpoints, devices // kpoints, 2, states, length)

time: 84.9 us -> 61.7 us (0.73)
  blocking collectives: 35.4 us -> 0 us
  Pallas kernels: 32.1 us -> 60.2 us
  starting transfers between devices: 8.53 us -> 0 us
  local copies, waits for them, and re-layouts: 4.88 us -> 1.29 us
  waiting for transfers between devices: 3.55 us -> 0 us
    all_gather x3 -> x0, blocking collectives: 35.4 us -> none  [the longest x1 21.2 us: body(): cols = lax.all_gather(cols, 'ka', axis=0, axis_index_groups=lines)]
    pallas_call x0 -> x1, Pallas kernels: none -> 28.1 us  [exchange(): pl.pallas_call(functools.partial(exchange_kernel, groups, n), out_shape=[...]
    all_to_all x2 -> x0, starting transfers between devices: 8.53 us -> none  [the longest x1 5.16 us: body(): rows = lax.all_to_all(rows, 'ka', 0, 0, axis_index_groups=lines, tiled=True)]
    all_to_all x2 -> x0, waiting for transfers between devices: 3.55 us -> none  [the longest x1 3.55 us: body(): lax.all_to_all(cols, 'ka', 0, 0, axis_index_groups=planes, tiled=True)]
    broadcast_in_dim x2 -> x0, local copies, waits for them, and re-layouts: 1.74 us -> none  [the longest x1 0.87 us: polarizability(): occ_weight[:, :, None]]
    all_gather x1 -> x0, local copies, waits for them, and re-layouts: 0.99 us -> none  [body(): rows = lax.all_gather(rows, 'ka', axis=0, axis_index_groups=planes)]
  transfers between devices with their start and end apart: 2 -> 0, of which waited for: 1 -> 0; matrix products, arithmetic and copies ran while one was open for 2% -> 0% of each run, Pallas kernels for 0% -> 0%
where the time goes in v1:
time: 61.7 us; the launch traced here: 61.5 us
  Pallas kernels  60.2 us (98%)
  local copies, waits for them, and re-layouts  1.29 us (2%)
    pallas_call x1, Pallas kernels, exchange(): pl.pallas_call(functools.partial(exchange_kernel, groups, n), out_shape=[...  28.1 us
    pallas_call x1, Pallas kernels, orbitals_at(): pl.pallas_call(functools.partial(orbital_kernel, chunk), grid=(NG // GROU...  18.5 us
    pallas_call x1, Pallas kernels, polarizability(): pl.pallas_call(polar_kernel, out_shape=jax.ShapeDtypeStruct((2, 1, row_le...  13.7 us
    reshape x1, local copies, waits for them, and re-layouts, orbitals_at(): points.reshape(1, total)  1.29 us

profile of v1, /device:TPU:0, one launch (start us, length us, event | category | flops | bytes accessed | tf_op | source)
XLA Modules:
  0.0 61.5 jit_solution(14907019336416793321)
XLA Ops:
  0.0 1.3 %reshape.3.pts_ref = s32[1,1536]{1,0:T(1,128)} reshape(s32[1536]{0:T(1024)} %param.9) | data formatting | bytes 12288 | tf_op jit(solution)/shard_map/reshape | solution.py:111
  1.3 18.5 %orbitals.1.own_ref = bf16[2,2,32,384]{3,2,1,0:T(8,128)(2,1)} custom-call(s32[1,1536]{1,0:T(1,128)} %reshape.3.pts_ref, bf16[2,32,32768]{2,1,0:T(8,128)(2,1)} %coef_ref.1), custom_call_target="tpu_custom_call" | custom-call | tf_op jit(solution)/shard_map/orbitals/pallas_call | solution.py:93
  19.7 28.1 %exchange.1 = (bf16[16,2,32,384]{3,2,1,0:T(8,128)(2,1)}, bf16[16,2,32,384]{3,2,1,0:T(8,128)(2,1)}, bf16[4,2,32,384]{3,2,1,0:T(8,128)(2,1)}) custom-call(bf16[2,2,32,384]{3,2,1,0:T(8,128)(2,1)} %orbitals.1.own_ref), custom_call_target="tpu_custom_call" | custom-call | tf_op jit(solution)/shard_map/exchange/pallas_call | solution.py:232
  47.8 13.7 %polarizability.1 = f32[2,1,384,384]{3,2,1,0:T(8,128)} custom-call(s32[16]{0:T(128)} %partner_ref.1, bf16[16,2,32,384]{3,2,1,0:T(8,128)(2,1)} %get-tuple-element.7.row_ref, bf16[16,2,32,384]{3,2,1,0:T(8,128)(2,1)} %get-tuple-element.8.col_ref, f32[16,32]{1,0:T(8,128)} %occ_ref.1, f32[16,32]{1,0:T(8,128)} %virt_ref.1), custom_call_target="tpu_custom_call" | custom-call | tf_op jit(solution)/shard_map/polarizability/pallas_call | solution.py:282

commit v2 on v1

--- a/solution.py
+++ b/solution.py
@@ -14,12 +14,22 @@
 VMEM_LIMIT = 56 * 1024 * 1024
 
 
+def cosine(phase):
+    folded = jnp.minimum(phase, NG - phase) - NG // 4
+    angle = folded.astype(jnp.float32) * (-2.0 * math.pi / NG)
+    square = angle * angle
+    total = jnp.full_like(square, 1.0 / math.factorial(13))
+    for order in range(11, 0, -2):
+        total = (-1.0) ** (order // 2) / math.factorial(order) + square * total
+    return angle * total
+
+
 def phase_rows(frequency, targets):
-    angles = ((frequency * targets) % NG).astype(jnp.float32) * (2.0 * math.pi / NG)
-    return jnp.cos(angles), jnp.sin(angles)
-
-
-def orbital_kernel(chunk, pts_ref, coef_ref, out_ref, lhs, cos_hi, sin_hi, cos_lo, sin_lo, xcos, xsin, acc):
+    phase = frequency * targets
+    return cosine(phase & (NG - 1)), cosine((phase - NG // 4) & (NG - 1))
+
+
+def orbital_kernel(chunk, pts_ref, coef_ref, out_ref, lhs, cos_table, sin_table, xcos, xsin, acc):
     step = pl.program_id(0)
     states = coef_ref.shape[1]
     count = acc.shape[2]
@@ -30,40 +40,38 @@
         pts = pts_ref[:, pl.ds(start, count)]
         frequency = lax.broadcasted_iota(jnp.int32, (NG, count), 0)
         norm = 1.0 / math.sqrt(NG**3)
-        cos_x, sin_x = phase_rows(frequency, pts // PLANE)
+        cos_x, sin_x = phase_rows(frequency, pts >> 10)
         xcos[...] = cos_x * norm
         xsin[...] = sin_x * norm
-        cos_y, sin_y = phase_rows(frequency, pts // NG % NG)
-        cos_z, sin_z = phase_rows(frequency, pts % NG)
+        cos_y, sin_y = phase_rows(frequency, (pts >> 5) & (NG - 1))
+        cos_z, sin_z = phase_rows(frequency, pts & (NG - 1))
         for gy in range(NG):
             rows = slice(gy * NG, (gy + 1) * NG)
             cy, sy = cos_y[gy : gy + 1], sin_y[gy : gy + 1]
             cos_t = cy * cos_z - sy * sin_z
             sin_t = sy * cos_z + cy * sin_z
-            high = cos_t.astype(jnp.bfloat16)
-            cos_hi[rows] = high
-            cos_lo[rows] = (cos_t - high.astype(jnp.float32)).astype(jnp.bfloat16)
-            high = sin_t.astype(jnp.bfloat16)
-            sin_hi[rows] = high
-            sin_lo[rows] = (sin_t - high.astype(jnp.float32)).astype(jnp.bfloat16)
+            low_rows = slice(PLANE + gy * NG, PLANE + (gy + 1) * NG)
+            for table, value in ((cos_table, cos_t), (sin_table, sin_t)):
+                high = value.astype(jnp.bfloat16)
+                table[rows] = high
+                table[low_rows] = (value - high.astype(jnp.float32)).astype(jnp.bfloat16)
         acc[...] = jnp.zeros_like(acc)
 
     for j in range(GROUP):
         for c in range(2):
             start = (2 * j + c) * states
-            lhs[start : start + states] = coef_ref[c, :, j * PLANE : (j + 1) * PLANE]
-
-    def dot(table, low, cols):
-        left = lhs[...]
-        return jnp.dot(left, table[:, cols], preferred_element_type=jnp.float32) + jnp.dot(
-            left, low[:, cols], preferred_element_type=jnp.float32
-        )
+            value = coef_ref[c, :, j * PLANE : (j + 1) * PLANE]
+            lhs[start : start + states, :PLANE] = value
+            lhs[start : start + states, PLANE:] = value
+
+    def dot(table, cols):
+        return jnp.dot(lhs[...], table[:, cols], preferred_element_type=jnp.float32)
 
     gx = pl.ds(pl.multiple_of(step * GROUP, GROUP), GROUP)
     for m in range(count // chunk):
         cols = slice(m * chunk, (m + 1) * chunk)
-        by_cos = dot(cos_hi, cos_lo, cols)
-        by_sin = dot(sin_hi, sin_lo, cols)
+        by_cos = dot(cos_table, cols)
+        by_sin = dot(sin_table, cols)
         pc, ps = xcos[gx, cols], xsin[gx, cols]
         real_sum, imag_sum = acc[0, :, cols], acc[1, :, cols]
         for j in range(GROUP):
@@ -88,7 +96,7 @@
     states = coefficients.shape[1]
     total = points.shape[0]
     chunk = 256 if count % 256 == 0 else 128
-    table = pltpu.VMEM((PLANE, count), jnp.bfloat16)
+    table = pltpu.VMEM((2 * PLANE, count), jnp.bfloat16)
     out_shape = (count // length, 2, states, length)
     return pl.pallas_call(
         functools.partial(orbital_kernel, chunk),
@@ -100,8 +108,8 @@
         ],
         out_specs=pl.BlockSpec(out_shape, lambda i: (0, 0, 0, 0)),
         scratch_shapes=[
-            pltpu.VMEM((GROUP * 2 * states, PLANE), jnp.bfloat16),
-            table, table, table, table,
+            pltpu.VMEM((GROUP * 2 * states, 2 * PLANE), jnp.bfloat16),
+            table, table,
             pltpu.VMEM((NG, count), jnp.float32),
             pltpu.VMEM((NG, count), jnp.float32),
             pltpu.VMEM((2, states, count), jnp.float32),
@@ -242,38 +250,49 @@
     return rows, cols
 
 
-def polar_kernel(partner_ref, row_ref, col_ref, occ_ref, virt_ref, out_ref):
-    kpoints, parts, bands, _ = row_ref.shape
+def polar_kernel(partner_ref, row_ref, col_ref, occ_ref, virt_ref, out_ref, right_ref, acc):
+    kpoints, parts, bands, row_len = row_ref.shape
+    col_len = col_ref.shape[3]
+    tile = col_len // 3 if col_len % 384 == 0 else col_len
     scaling = 1.0 / (bands * bands)
-    dims = (((0,), (0,)), ((), ()))
-
     diagonal = lax.broadcasted_iota(jnp.int32, (bands, bands), 0) == lax.broadcasted_iota(
         jnp.int32, (bands, bands), 1
     )
 
-    def density(k, weight_ref):
-        rows = row_ref[k].astype(jnp.float32)
+    def left(k, weight_ref):
         weight = jnp.where(diagonal, weight_ref[pl.ds(k, 1), :], 0.0)
         weight = jnp.sum(weight, axis=1, keepdims=True)
-        weighted = (rows * weight[None]).astype(jnp.bfloat16)
+        weighted = (row_ref[k].astype(jnp.float32) * weight[None]).astype(jnp.bfloat16)
+        real, imag = weighted[0], weighted[1]
+        return jnp.concatenate([real, imag], axis=0), jnp.concatenate([imag, -real], axis=0)
+
+    def turn(k, carry):
         cols = col_ref[k]
-        right = jnp.concatenate([cols[0], cols[1]], axis=0)
-        real_left = jnp.concatenate([weighted[0], weighted[1]], axis=0)
-        imag_left = jnp.concatenate([weighted[1], -weighted[0]], axis=0)
-        return (
-            lax.dot_general(real_left, right, dims, preferred_element_type=jnp.float32),
-            lax.dot_general(imag_left, right, dims, preferred_element_type=jnp.float32),
-        )
+        right_ref[k] = jnp.concatenate([cols[0], cols[1]], axis=0).T
+        return carry
 
     def step(k, carry):
-        occ_real, occ_imag = density(k, occ_ref)
-        virt_real, virt_imag = density(partner_ref[k], virt_ref)
-        out_ref[0, 0] += (occ_real * virt_real + occ_imag * virt_imag) * scaling
-        out_ref[1, 0] += (occ_imag * virt_real - occ_real * virt_imag) * scaling
+        other = partner_ref[k]
+        occ_left = left(k, occ_ref)
+        virt_left = left(other, virt_ref)
+        for m in range(col_len // tile):
+            rows = slice(m * tile, (m + 1) * tile)
+            occ_right, virt_right = right_ref[k, rows], right_ref[other, rows]
+            occ_real, occ_imag = [
+                jnp.dot(occ_right, value, preferred_element_type=jnp.float32) for value in occ_left
+            ]
+            virt_real, virt_imag = [
+                jnp.dot(virt_right, value, preferred_element_type=jnp.float32) for value in virt_left
+            ]
+            acc[0, rows] += occ_real * virt_real + occ_imag * virt_imag
+            acc[1, rows] += occ_imag * virt_real - occ_real * virt_imag
         return carry
 
-    out_ref[...] = jnp.zeros_like(out_ref)
+    acc[...] = jnp.zeros_like(acc)
+    lax.fori_loop(0, kpoints, turn, 0)
     lax.fori_loop(0, kpoints, step, 0)
+    for c in range(parts):
+        out_ref[c, 0] = acc[c].T * scaling
 
 
 def polarizability(partner, row_side, col_side, occ_weight, virt_weight):
@@ -284,6 +303,10 @@
         out_shape=jax.ShapeDtypeStruct((2, 1, row_len, col_len), jnp.float32),
         in_specs=[pl.BlockSpec(memory_space=pltpu.SMEM), vmem, vmem, vmem, vmem],
         out_specs=vmem,
+        scratch_shapes=[
+            pltpu.VMEM((col_side.shape[0], col_len, 2 * col_side.shape[2]), jnp.bfloat16),
+            pltpu.VMEM((2, col_len, row_len), jnp.float32),
+        ],
         compiler_params=pltpu.CompilerParams(vmem_limit_bytes=VMEM_LIMIT),
         name="polarizability",
     )(partner, row_side, col_side, occ_weight, virt_weight)

time: 61.7 us -> 60.6 us (0.982)
  Pallas kernels: 60.2 us -> 59.1 us
    pallas_call x1, Pallas kernels: 18.5 us -> 17.7 us  [orbitals_at(): pl.pallas_call(functools.partial(orbital_kernel, chunk), grid=(NG // GROU...]
where the time goes in v2:
time: 60.6 us; the launch traced here: 60.4 us
  Pallas kernels  59.1 us (98%)
  local copies, waits for them, and re-layouts  1.29 us (2%)
    pallas_call x1, Pallas kernels, exchange(): pl.pallas_call(functools.partial(exchange_kernel, groups, n), out_shape=[...  28.1 us
    pallas_call x1, Pallas kernels, orbitals_at(): pl.pallas_call(functools.partial(orbital_kernel, chunk), grid=(NG // GROU...  17.7 us
    pallas_call x1, Pallas kernels, polarizability(): pl.pallas_call(polar_kernel, out_shape=jax.ShapeDtypeStruct((2, 1, row_le...  13.3 us
    reshape x1, local copies, waits for them, and re-layouts, orbitals_at(): points.reshape(1, total)  1.29 us

profile of v2, /device:TPU:0, one launch (start us, length us, event | category | flops | bytes accessed | tf_op | source)
XLA Modules:
  0.0 60.4 jit_solution(14160792630273757163)
XLA Ops:
  0.0 1.3 %reshape.3.pts_ref = s32[1,1536]{1,0:T(1,128)} reshape(s32[1536]{0:T(1024)} %param.9) | data formatting | bytes 12288 | tf_op jit(solution)/shard_map/reshape | solution.py:119
  1.3 17.7 %orbitals.1.own_ref = bf16[2,2,32,384]{3,2,1,0:T(8,128)(2,1)} custom-call(s32[1,1536]{1,0:T(1,128)} %reshape.3.pts_ref, bf16[2,32,32768]{2,1,0:T(8,128)(2,1)} %coef_ref.1), custom_call_target="tpu_custom_call" | custom-call | tf_op jit(solution)/shard_map/orbitals/pallas_call | solution.py:101
  19.0 28.1 %exchange.1 = (bf16[16,2,32,384]{3,2,1,0:T(8,128)(2,1)}, bf16[16,2,32,384]{3,2,1,0:T(8,128)(2,1)}, bf16[4,2,32,384]{3,2,1,0:T(8,128)(2,1)}) custom-call(bf16[2,2,32,384]{3,2,1,0:T(8,128)(2,1)} %orbitals.1.own_ref), custom_call_target="tpu_custom_call" | custom-call | tf_op jit(solution)/shard_map/exchange/pallas_call | solution.py:240
  47.1 13.3 %polarizability.1 = f32[2,1,384,384]{3,2,1,0:T(8,128)} custom-call(s32[16]{0:T(128)} %partner_ref.1, bf16[16,2,32,384]{3,2,1,0:T(8,128)(2,1)} %get-tuple-element.7.row_ref, bf16[16,2,32,384]{3,2,1,0:T(8,128)(2,1)} %get-tuple-element.8.col_ref, f32[16,32]{1,0:T(8,128)} %occ_ref.1, f32[16,32]{1,0:T(8,128)} %virt_ref.1), custom_call_target="tpu_custom_call" | custom-call | tf_op jit(solution)/shard_map/polarizability/pallas_call | solution.py:301

commit v3 on v2

--- a/solution.py
+++ b/solution.py
@@ -234,14 +234,14 @@
 
 def exchange(own, groups, devices, n):
     _, _, states, length = own.shape
-    anywhere = pl.BlockSpec(memory_space=pl.ANY)
+    inside = pl.BlockSpec(memory_space=pltpu.VMEM)
     side = jax.ShapeDtypeStruct((devices, 2, states, length), jnp.bfloat16)
     sem = pltpu.SemaphoreType.DMA
     rows, cols, _ = pl.pallas_call(
         functools.partial(exchange_kernel, groups, n),
         out_shape=[side, side, jax.ShapeDtypeStruct((n, 2, states, length), jnp.bfloat16)],
-        in_specs=[anywhere],
-        out_specs=[anywhere] * 3,
+        in_specs=[inside],
+        out_specs=[inside] * 3,
         scratch_shapes=[sem((3,)), sem((groups,)), sem((groups,))]
         + [sem((n,))] * 4 + [sem((n, n))] * 6,
         compiler_params=pltpu.CompilerParams(collective_id=0, has_side_effects=True),

time: 60.6 us -> 61.7 us (1.018)
  Pallas kernels: 59.1 us -> 60.2 us
    pallas_call x1, Pallas kernels: 28.1 us -> 29.1 us  [exchange(): pl.pallas_call(functools.partial(exchange_kernel, groups, n), out_shape=[...]
where the time goes in v3:
time: 61.7 us; the launch traced here: 61.5 us
  Pallas kernels  60.2 us (98%)
  local copies, waits for them, and re-layouts  1.29 us (2%)
    pallas_call x1, Pallas kernels, exchange(): pl.pallas_call(functools.partial(exchange_kernel, groups, n), out_shape=[...  29.1 us
    pallas_call x1, Pallas kernels, orbitals_at(): pl.pallas_call(functools.partial(orbital_kernel, chunk), grid=(NG // GROU...  17.7 us
    pallas_call x1, Pallas kernels, polarizability(): pl.pallas_call(polar_kernel, out_shape=jax.ShapeDtypeStruct((2, 1, row_le...  13.3 us
    reshape x1, local copies, waits for them, and re-layouts, orbitals_at(): points.reshape(1, total)  1.29 us

profile of v3, /device:TPU:0, one launch (start us, length us, event | category | flops | bytes accessed | tf_op | source)
XLA Modules:
  0.0 61.5 jit_solution(5018829517929295143)
XLA Ops:
  0.0 1.3 %reshape.3.pts_ref = s32[1,1536]{1,0:T(1,128)} reshape(s32[1536]{0:T(1024)} %param.9) | data formatting | bytes 12288 | tf_op jit(solution)/shard_map/reshape | solution.py:119
  1.3 17.7 %orbitals.1.own_ref = bf16[2,2,32,384]{3,2,1,0:T(8,128)(2,1)} custom-call(s32[1,1536]{1,0:T(1,128)} %reshape.3.pts_ref, bf16[2,32,32768]{2,1,0:T(8,128)(2,1)} %coef_ref.1), custom_call_target="tpu_custom_call" | custom-call | tf_op jit(solution)/shard_map/orbitals/pallas_call | solution.py:101
  19.0 29.1 %exchange.1 = (bf16[16,2,32,384]{3,2,1,0:T(8,128)(2,1)}, bf16[16,2,32,384]{3,2,1,0:T(8,128)(2,1)}, bf16[4,2,32,384]{3,2,1,0:T(8,128)(2,1)}) custom-call(bf16[2,2,32,384]{3,2,1,0:T(8,128)(2,1)} %orbitals.1.own_ref), custom_call_target="tpu_custom_call" | custom-call | tf_op jit(solution)/shard_map/exchange/pallas_call | solution.py:240
  48.1 13.3 %polarizability.1 = f32[2,1,384,384]{3,2,1,0:T(8,128)} custom-call(s32[16]{0:T(128)} %partner_ref.1, bf16[16,2,32,384]{3,2,1,0:T(8,128)(2,1)} %get-tuple-element.7.row_ref, bf16[16,2,32,384]{3,2,1,0:T(8,128)(2,1)} %get-tuple-element.8.col_ref, f32[16,32]{1,0:T(8,128)} %occ_ref.1, f32[16,32]{1,0:T(8,128)} %virt_ref.1), custom_call_target="tpu_custom_call" | custom-call | tf_op jit(solution)/shard_map/polarizability/pallas_call | solution.py:301

commit v4 on v2

--- a/solution.py
+++ b/solution.py
@@ -290,7 +290,7 @@
 
     acc[...] = jnp.zeros_like(acc)
     lax.fori_loop(0, kpoints, turn, 0)
-    lax.fori_loop(0, kpoints, step, 0)
+    lax.fori_loop(0, kpoints, step, 0, unroll=4)
     for c in range(parts):
         out_ref[c, 0] = acc[c].T * scaling
 

time: 60.6 us -> 58.1 us (0.959)
  Pallas kernels: 59.1 us -> 56.6 us
    pallas_call x1, Pallas kernels: 13.3 us -> 10.8 us  [polarizability(): pl.pallas_call(polar_kernel, out_shape=jax.ShapeDtypeStruct((2, 1, row_le...]
where the time goes in v4:
time: 58.1 us; the launch traced here: 57.9 us
  Pallas kernels  56.6 us (97%)
  local copies, waits for them, and re-layouts  1.29 us (2%)
    pallas_call x1, Pallas kernels, exchange(): pl.pallas_call(functools.partial(exchange_kernel, groups, n), out_shape=[...  28.1 us
    pallas_call x1, Pallas kernels, orbitals_at(): pl.pallas_call(functools.partial(orbital_kernel, chunk), grid=(NG // GROU...  17.7 us
    pallas_call x1, Pallas kernels, polarizability(): pl.pallas_call(polar_kernel, out_shape=jax.ShapeDtypeStruct((2, 1, row_le...  10.8 us
    reshape x1, local copies, waits for them, and re-layouts, orbitals_at(): points.reshape(1, total)  1.29 us

profile of v4, /device:TPU:0, one launch (start us, length us, event | category | flops | bytes accessed | tf_op | source)
XLA Modules:
  0.0 57.9 jit_solution(1090928282072666523)
XLA Ops:
  0.0 1.3 %reshape.3.pts_ref = s32[1,1536]{1,0:T(1,128)} reshape(s32[1536]{0:T(1024)} %param.9) | data formatting | bytes 12288 | tf_op jit(solution)/shard_map/reshape | solution.py:119
  1.3 17.7 %orbitals.1.own_ref = bf16[2,2,32,384]{3,2,1,0:T(8,128)(2,1)} custom-call(s32[1,1536]{1,0:T(1,128)} %reshape.3.pts_ref, bf16[2,32,32768]{2,1,0:T(8,128)(2,1)} %coef_ref.1), custom_call_target="tpu_custom_call" | custom-call | tf_op jit(solution)/shard_map/orbitals/pallas_call | solution.py:101
  19.0 28.1 %exchange.1 = (bf16[16,2,32,384]{3,2,1,0:T(8,128)(2,1)}, bf16[16,2,32,384]{3,2,1,0:T(8,128)(2,1)}, bf16[4,2,32,384]{3,2,1,0:T(8,128)(2,1)}) custom-call(bf16[2,2,32,384]{3,2,1,0:T(8,128)(2,1)} %orbitals.1.own_ref), custom_call_target="tpu_custom_call" | custom-call | tf_op jit(solution)/shard_map/exchange/pallas_call | solution.py:240
  47.1 10.8 %polarizability.1 = f32[2,1,384,384]{3,2,1,0:T(8,128)} custom-call(s32[16]{0:T(128)} %partner_ref.1, bf16[16,2,32,384]{3,2,1,0:T(8,128)(2,1)} %get-tuple-element.7.row_ref, bf16[16,2,32,384]{3,2,1,0:T(8,128)(2,1)} %get-tuple-element.8.col_ref, f32[16,32]{1,0:T(8,128)} %occ_ref.1, f32[16,32]{1,0:T(8,128)} %virt_ref.1), custom_call_target="tpu_custom_call" | custom-call | tf_op jit(solution)/shard_map/polarizability/pallas_call | solution.py:301
